TPU v7x, 32 devices: a whole 2x2x4 slice. The times are simulated.
32 devices in a mesh: row: 4 (over z), col: 8 (over y, x, core).
Axes of the slice: x: 2, y: 2, z: 4, core: 2. Of those that a mesh axis runs over, the one named last changes fastest.
Arguments:
- rhs_atlas: float32 [32768, 4096], P('row', 'col'), may hold values from -6 to 6
- tile_block: int32 [64], replicated, may hold values from 0 to 63, as said below
- panels: float32 [2, 512, 32768], P(None, 'col', 'row'), may hold values from -0.1875 to 0.1875
- diag_inverse: float32 [2, 512, 512], replicated, as said below
Outputs:
- solved: float32 [2, 512, 4096], P(None, None, 'col')
- trailing: float32 [32768, 4096], P('row', 'col')
Inputs may be any that keep to these rules, and one draw needn't show every extreme that they name: tile_block is a permutation of 0 to 63, and each aligned block of 16 entries holds exactly 4 entries of every residue modulo 4. `diag_inverse`: each matrix is lower triangular with diagonal entries between 0.5 and 1.5.
All inputs are finite; a program needn't handle non-finite values.
Results may differ from a plain program's by a relative error of at most 0.00008.
Values sent between devices are 32-bit elements; how exact they have to be, the bound alone decides.
No kernel may reach another device: no remote copies, remote signals or barrier semaphores. Data moves between devices by JAX's collectives and lax.ppermute only.
A program may use at most 128 MiB of HBM per device.

v0:
```python
import jax
import jax.numpy as jnp
from jax import lax
from jax.sharding import PartitionSpec as P


def from_root(x, axis, root):
    mine = lax.axis_index(axis) == root
    return lax.psum(jnp.where(mine, x, jnp.zeros_like(x)), axis)


def solve_block(which, leading, diag_inverse):
    local_solve = jnp.dot(
        diag_inverse[which],
        leading,
        precision=lax.Precision.HIGHEST,
        preferred_element_type=jnp.float32,
    )
    return from_root(local_solve, "row", which)


def panel_update(which, panels, keeps, solution):
    masked = panels[which] * keeps[which][None, :]
    return lax.dot_general(
        lax.all_gather(masked, "col", axis=0, tiled=True),
        solution,
        (((0,), (0,)), ((), ())),
        precision=lax.Precision.HIGHEST,
        preferred_element_type=jnp.float32,
    )


def shards(rhs_atlas, tile_block, panels, diag_inverse):
    rows_axis = lax.axis_size("row")
    mine_row = lax.axis_index("row")
    block = diag_inverse.shape[1]
    width = rhs_atlas.shape[1]
    local_blocks = rhs_atlas.shape[0] // block
    total_blocks = tile_block.shape[0]
    tiles = rhs_atlas.reshape(local_blocks, block, width)
    my_tiles = lax.dynamic_slice_in_dim(tile_block, mine_row * local_blocks, local_blocks)
    send_order = jnp.argsort(my_tiles % rows_axis, stable=True)
    outgoing = jnp.take(tiles, send_order, axis=0)
    incoming = lax.all_to_all(outgoing, "row", split_axis=0, concat_axis=0, tiled=True)
    every_tile = jnp.arange(total_blocks, dtype=jnp.int32)
    ranked = jnp.where(tile_block % rows_axis == mine_row, every_tile, total_blocks)
    picked = jnp.argsort(ranked)[:local_blocks]
    local_index = jnp.take(tile_block, picked) // rows_axis
    placing = jnp.argsort(local_index)
    blocks = jnp.take(incoming, placing, axis=0)
    flat = blocks.reshape(local_blocks * block, width)
    block_ids = jnp.arange(local_blocks, dtype=jnp.int32) * rows_axis + mine_row
    row_block = jnp.repeat(block_ids, block)
    keeps = jnp.stack([(row_block > 0).astype(jnp.float32), (row_block > 1).astype(jnp.float32)])
    first = solve_block(0, flat[:block], diag_inverse)
    flat = flat - panel_update(0, panels, keeps, first)
    second = solve_block(1, flat[:block], diag_inverse)
    flat = flat - panel_update(1, panels, keeps, second)
    return (jnp.stack([first, second]), flat)


def solution(mesh):
    placed = (P("row", "col"), P(), P(None, "col", "row"), P())
    return jax.shard_map(
        shards,
        mesh=mesh,
        in_specs=placed,
        out_specs=(P(None, None, "col"), P("row", "col")),
        check_vma=False,
    )
```

profile of v0, /device:TPU:18, one launch (start us, length us, event | category | flops | bytes accessed | tf_op | source)
XLA Modules:
  0.0 767.8 jit_solution(10429845087136344704)
XLA Ops:
  8.0 0.7 and_select_fusion.3
  8.7 1.2 sort.51
  10.0 14.3 %gather_fusion.1 = f32[16,512,512]{2,1,0:T(8,128)} fusion(f32[16,512,512]{2,1,0:T(8,128)} %bitcast.32, s32[1024]{0:T(1024)S(1)} %pad_clamp_fusion.1), kind=kCustom, calls=%fused_computation.clone | custom fusion | bytes 33554496 | tf_op jit(solution)/shard_map/jit(_take)/gather | solution.py:43
  24.3 12.1 %broadcast_select_fusion.1 = f32[16,512,512]{2,1,0:T(8,128)} fusion(f32[16,512,512]{2,1,0:T(8,128)} %gather_fusion.1, pred[16]{0:T(512)(128)(4,1)S(1)} %compare_and_fusion.1), kind=kLoop, calls=%fused_computation.6 | loop fusion | flops 4194304 | bytes 33554448 | tf_op jit(solution)/shard_map/jit(_take)/select_n | solution.py:43
  36.4 0.0 copy-start
  36.4 7.4 all-to-all-start
  43.8 0.0 all-reduce.3.cloned.1.call-start
  43.8 0.0 copy-done
  43.8 2.0 sort.52
  45.8 0.7 gather_fusion
  46.5 0.1 broadcast_bitcast_fusion.1
  46.6 0.1 broadcast_bitcast_fusion
  46.7 1.2 sort.53
  48.0 355.6 %all-to-all-done = f32[16,512,512]{2,1,0:T(8,128)} async-done(((f32[16,512,512]{2,1,0:T(8,128)}), f32[16,512,512]{2,1,0:T(8,128)}, u32[]{:S(2)}, u32[]{:S(2)}) %all-to-all-start) | async-done | bytes 16777248 | tf_op jit(solution)/shard_map/all_to_all | solution.py:44
  403.6 14.3 %gather_fusion.2 = f32[16,512,512]{2,1,0:T(8,128)} fusion(f32[16,512,512]{2,1,0:T(8,128)} %all-to-all-done, s32[1024]{0:T(1024)S(1)} %pad_clamp_fusion), kind=kCustom, calls=%fused_computation.1.clone | custom fusion | bytes 33554496 | tf_op jit(solution)/shard_map/jit(_take)/gather | solution.py:50
  417.8 0.0 copy-start.4
  417.8 7.8 %broadcast_select_fusion = f32[16,512,512]{2,1,0:T(8,128)S(1)} fusion(f32[16,512,512]{2,1,0:T(8,128)} %gather_fusion.2, pred[16]{0:T(512)(128)(4,1)S(1)} %compare_and_fusion), kind=kLoop, calls=%fused_computation.5 | loop fusion | flops 4194304 | bytes 33554448 | tf_op jit(solution)/shard_map/jit(_take)/select_n | solution.py:50
  425.6 0.0 copy-start.2
  425.6 6.2 copy-done.2
  431.8 0.0 copy-done.4
  431.8 4.5 fusion.1
  436.2 0.0 all-reduce.3.cloned.1.call-update
  436.3 0.0 all-gather.3.cloned.1.call-start
  436.3 4.7 bitcast_multiply_fusion
  441.0 0.0 all-gather.3.cloned.1.call-update
  441.0 0.0 all-reduce.5.cloned.1.call-start
  441.0 48.5 %all-reduce.3.cloned.1.call-done = f32[512,512]{0,1:T(8,128)} async-done(((f32[512,512]{0,1:T(8,128)}), f32[512,512]{0,1:T(8,128)}) %all-reduce.3.cloned.1.call-update) | async-done | bytes 1048592 | tf_op jit(solution)/shard_map/psum | solution.py:9
  489.5 0.0 copy-start.3
  489.5 43.2 %all-gather.3.cloned.1.call-done = f32[512,8192]{1,0:T(8,128)} async-done(((f32[64,8192]{1,0:T(8,128)}), f32[512,8192]{1,0:T(8,128)}) %all-gather.3.cloned.1.call-update) | async-done | bytes 16777232 | tf_op jit(solution)/shard_map/all_gather | solution.py:25
  532.7 56.8 %bitcast_subtract_fusion = f32[8192,512]{1,0:T(8,128)S(1)} fusion(f32[16,512,512]{2,1,0:T(8,128)} %copy-done.2, f32[512,8192]{1,0:T(8,128)} %all-gather.3.cloned.1.call-done, f32[512,512]{0,1:T(8,128)} %all-reduce.3.cloned.1.call-done), kind=kOutput, calls=%fused_computation.3 | convolution fusion | flops 25773998080 | bytes 51380224 | tf_op jit(solution)/shard_map/dot_general | solution.py:24
  589.5 0.0 copy-start.1
  589.5 6.2 copy-done.1
  595.7 4.4 fusion
  600.1 0.0 all-reduce.5.cloned.1.call-update
  600.1 0.0 all-gather.5.cloned.1.call-start
  600.2 0.5 all-gather.5.cloned.1.call-update
  600.7 50.8 %all-reduce.5.cloned.1.call-done = f32[512,512]{0,1:T(8,128)} async-done(((f32[512,512]{0,1:T(8,128)}), f32[512,512]{0,1:T(8,128)}) %all-reduce.5.cloned.1.call-update) | async-done | bytes 1048592 | tf_op jit(solution)/shard_map/psum | solution.py:9
  651.5 0.0 copy-done.3
  651.5 1.4 pad_maximum_fusion
  652.9 1.8 copy.7
  654.7 37.5 %all-gather.5.cloned.1.call-done = f32[512,8192]{1,0:T(8,128)} async-done(((f32[64,8192]{1,0:T(8,128)}), f32[512,8192]{1,0:T(8,128)}) %all-gather.5.cloned.1.call-update) | async-done | bytes 16777232 | tf_op jit(solution)/shard_map/all_gather | solution.py:25
  692.2 68.0 %convolution_subtract_fusion = f32[8192,512]{1,0:T(8,128)} fusion(f32[8192,512]{1,0:T(8,128)} %copy-done.1, f32[512,8192]{1,0:T(8,128)} %all-gather.5.cloned.1.call-done, f32[512,512]{0,1:T(8,128)} %all-reduce.5.cloned.1.call-done), kind=kOutput, calls=%fused_computation.4 | convolution fusion | flops 25773998080 | bytes 51380224 | tf_op jit(solution)/shard_map/dot_general | solution.py:24
  (16 shorter events, 0.1 us)
Async XLA Ops:
  36.4 7.4 copy-start
  36.4 367.2 %all-to-all-start = ((f32[16,512,512]{2,1,0:T(8,128)}), f32[16,512,512]{2,1,0:T(8,128)}, u32[]{:S(2)}, u32[]{:S(2)}) async-start(f32[16,512,512]{2,1,0:T(8,128)} %broadcast_select_fusion.1), calls=%async_computation | async-start | bytes 33554432 | tf_op jit(solution)/shard_map/all_to_all | solution.py:44
  43.8 445.8 %all-reduce.3.cloned.1.call-start = ((), (), s32[]{:S(2)}) async-start(), calls=%async_computation.1 | async-start | bytes 2097152 | tf_op jit(solution)/shard_map/psum | solution.py:9
  417.8 13.9 %copy-start.4 = (f32[2,512,512]{2,1,0:T(8,128)S(1)}, f32[2,512,512]{2,1,0:T(8,128)}, u32[]{:S(2)}) copy-start(f32[2,512,512]{2,1,0:T(8,128)} %param.9) | copy-start | bytes 6291460
  425.6 6.2 copy-start.2
  436.3 96.5 %all-gather.3.cloned.1.call-start = ((), (), s32[]{:S(2)}) async-start(), calls=%async_computation.2 | async-start | bytes 18874368 | tf_op jit(solution)/shard_map/all_gather | solution.py:25
  441.0 210.5 %all-reduce.5.cloned.1.call-start = ((), (), s32[]{:S(2)}) async-start(), calls=%async_computation.3 | async-start | bytes 2097152 | tf_op jit(solution)/shard_map/psum | solution.py:9
  489.5 162.0 %copy-start.3 = (f32[512,512]{0,1:T(8,128)S(1)}, f32[512,512]{0,1:T(8,128)}, u32[]{:S(2)}) copy-start(f32[512,512]{0,1:T(8,128)} %all-reduce.3.cloned.1.call-done) | copy-start | bytes 3145732
  589.5 6.2 copy-start.1
  600.1 92.1 %all-gather.5.cloned.1.call-start = ((), (), s32[]{:S(2)}) async-start(), calls=%async_computation.4 | async-start | bytes 18874368 | tf_op jit(solution)/shard_map/all_gather | solution.py:25
Sparse Core Ops, SparseCore 0:
  436.4 53.1 all-reduce.2
  600.3 51.1 all-reduce.4
Sparse Core Ops, SparseCore 1:
  441.1 91.6 all-gather.2
  602.5 89.7 all-gather.4
where the time goes:
time: 777 us; the launch traced here: 768 us
  waiting for transfers between devices  536 us (69%)
  matrix products  134 us (17%)
  local copies, waits for them, and re-layouts  43.5 us (6%)
  other arithmetic  31.2 us (4%)
  between operations  15.8 us (2%)
    all_to_all x1, waiting for transfers between devices, shards(): lax.all_to_all(outgoing, 'row', split_axis=0, concat_axis=0, tiled=True)  356 us
    dot_general x2, matrix products, panel_update(): lax.dot_general(lax.all_gather(masked, 'col', axis=0, tiled=True), soluti...  125 us
    psum x2, waiting for transfers between devices, from_root(): return lax.psum(jnp.where(mine, x, jnp.zeros_like(x)), axis)  99.3 us
    all_gather x2, waiting for transfers between devices, panel_update(): lax.all_gather(masked, 'col', axis=0, tiled=True)  80.7 us
  transfers between devices with their start and end apart: 5, of which 5 were waited for; matrix products, arithmetic and copies ran while one was open for 2% of the time, Pallas kernels for 0%

commit v1 on v0

v1 whole, which is shorter than its diff:
```python
import jax
import jax.numpy as jnp
from jax import lax
from jax.experimental import pallas as pl
from jax.experimental.pallas import tpu as pltpu
from jax.sharding import PartitionSpec as P

HIGHEST = lax.Precision.HIGHEST
HIGH = lax.Precision.HIGH
ANY = pl.BlockSpec(memory_space=pl.ANY)
SMEM = pl.BlockSpec(memory_space=pltpu.SMEM)


def ring(rows, shift):
    return [(i, (i + shift) % rows) for i in range(rows)]


def partners(rows, bit):
    return [(i, i ^ bit) for i in range(rows)]


def after(x, *events):
    return lax.optimization_barrier((x, *events))[0]


def mul(a, b, precision):
    return jnp.dot(a, b, precision=precision, preferred_element_type=jnp.float32)


def mul_t(a, b, precision):
    return lax.dot_general(
        a, b, (((0,), (0,)), ((), ())), precision=precision, preferred_element_type=jnp.float32
    )


def f32(*shape):
    return jax.ShapeDtypeStruct(shape, jnp.float32)


def opening(rows, first_shift, tiles, tile_block, panels, me):
    local, block, width = tiles.shape
    share = local // rows
    depth = panels.shape[1]
    half = block // 2
    chunks = block // width
    extra = depth * chunks // 2
    if chunks == 1:
        pieces = [[(0, h * extra, extra, 0)] for h in range(2)]
    else:
        pieces = [
            [(h * (chunks // 2) + k, 0, depth, k * depth) for k in range(chunks // 2)] for h in range(2)
        ]

    def kernel(block_ref, me_ref, tiles_ref, panels_ref, keep_ref, give_ref, sent_ref, order_ref, slots_ref, count, tile, halves, sem):
        me = me_ref[0]
        for shift in range(rows):
            count[shift] = 0

        def scan_mine(t, carry):
            shift = lax.rem(lax.rem(block_ref[me * local + t], rows) - me + rows, rows)
            seen = count[shift]
            order_ref[shift * share + seen] = t
            count[shift] = seen + 1
            return carry

        lax.fori_loop(0, local, scan_mine, 0)
        first_in = pltpu.make_async_copy(tiles_ref.at[order_ref[first_shift * share]], tile, sem.at[0])
        first_out = pltpu.make_async_copy(tile, sent_ref.at[0], sem.at[0])
        first_in.start()

        def find(t, carry):
            value = block_ref[t]
            return tuple(jnp.where(value == p, t, carry[p]) for p in range(2))

        at = lax.fori_loop(0, rows * local, find, (jnp.int32(0), jnp.int32(0)))
        bit0 = lax.rem(me, 2)

        def raw_in(p, k):
            start = pl.multiple_of((bit0 if k == 0 else 1 - bit0) * half, half)
            return pltpu.make_async_copy(
                tiles_ref.at[lax.rem(at[p], local), pl.ds(start, half)],
                halves.at[k, pl.ds(p * half, half)],
                sem.at[1 + 2 * p + k],
            )

        def corner_in(k, h):
            return [
                pltpu.make_async_copy(
                    panels_ref.at[0, pl.ds(start, size), pl.ds(chunk * width, width)],
                    halves.at[k, pl.ds(2 * half + to, size)],
                    sem.at[5 + k],
                )
                for chunk, start, size, to in pieces[h]
            ]

        for p in range(2):
            mine = at[p] // local == me

            @pl.when(mine)
            def _():
                for k in range(2):
                    raw_in(p, k).start()

            @pl.when(jnp.logical_not(mine))
            def _():
                for k in range(2):
                    halves[k, p * half : (p + 1) * half] = jnp.zeros((half, width), jnp.float32)

        for k in range(2):
            for h in range(2):

                @pl.when(jnp.logical_and(me == 1, bit0 == (h if k == 0 else 1 - h)))
                def _():
                    for copy in corner_in(k, h):
                        copy.start()

            @pl.when(me != 1)
            def _():
                halves[k, 2 * half :] = jnp.zeros((extra, width), jnp.float32)

        first_in.wait()
        first_out.start()
        for p in range(2):

            @pl.when(at[p] // local == me)
            def _():
                for k in range(2):
                    raw_in(p, k).wait()

        for k in range(2):

            @pl.when(me == 1)
            def _():
                for copy in corner_in(k, 0):
                    copy.wait()

        outs = [pltpu.make_async_copy(halves.at[k], ref, sem.at[1 + k]) for k, ref in enumerate((keep_ref, give_ref))]
        for copy in outs:
            copy.start()

        for shift in range(rows):
            source = lax.rem(me - shift + rows, rows)

            def scan_source(t, seen):
                value = block_ref[source * local + t]
                slots_ref[shift * share + seen] = value // rows
                return seen + (lax.rem(value, rows) == me).astype(jnp.int32)

            lax.fori_loop(0, local, scan_source, jnp.int32(0))
        first_out.wait()
        for copy in outs:
            copy.wait()

    return pl.pallas_call(
        kernel,
        out_shape=(
            f32(2 * half + extra, width),
            f32(2 * half + extra, width),
            f32(1, block, width),
            jax.ShapeDtypeStruct((local,), jnp.int32),
            jax.ShapeDtypeStruct((local + 8,), jnp.int32),
        ),
        in_specs=[SMEM, SMEM, ANY, ANY],
        out_specs=(ANY, ANY, ANY, SMEM, SMEM),
        scratch_shapes=[
            pltpu.SMEM((rows,), jnp.int32),
            pltpu.VMEM((block, width), jnp.float32),
            pltpu.VMEM((2, 2 * half + extra, width), jnp.float32),
            pltpu.SemaphoreType.DMA((7,)),
        ],
        cost_estimate=pl.CostEstimate(flops=0, bytes_accessed=6 << 20, transcendentals=0),
        name="opening",
    )(tile_block, me, tiles, panels)


def pack(plan, share, tiles, order):
    local, block, width = tiles.shape
    total = sum(hi - lo for _, lo, hi in plan)

    def kernel(order_ref, tiles_ref, *rest):
        sents, held, sem = rest[:-2], rest[-2], rest[-1]
        ins, outs = [], []
        for (shift, lo, hi), sent in zip(plan, sents):
            for c in range(lo, hi):
                n = len(ins)
                ins.append(
                    pltpu.make_async_copy(tiles_ref.at[order_ref[shift * share + c]], held.at[n], sem.at[n])
                )
                outs.append(pltpu.make_async_copy(held.at[n], sent.at[c - lo], sem.at[n]))
        for copy in ins:
            copy.start()
        for arrive, leave in zip(ins, outs):
            arrive.wait()
            leave.start()
        for copy in outs:
            copy.wait()

    return pl.pallas_call(
        kernel,
        out_shape=tuple(f32(hi - lo, block, width) for _, lo, hi in plan),
        in_specs=[SMEM, ANY],
        out_specs=tuple(ANY for _ in plan),
        scratch_shapes=[pltpu.VMEM((total, block, width), jnp.float32), pltpu.SemaphoreType.DMA((total,))],
        compiler_params=pltpu.CompilerParams(vmem_limit_bytes=32 << 20),
        cost_estimate=pl.CostEstimate(flops=0, bytes_accessed=8 * total * block * width, transcendentals=0),
        name="pack",
    )(order, tiles)


def settle(acc, source, slots, slot_at, count, order=None):
    local, block, width = acc.shape
    part = block // 2

    def kernel(slots_ref, order_ref, tile_ref, old_ref, new_ref):
        new_ref[...] = tile_ref[...] - old_ref[...]

    def at_tile(i, j, slots_ref, order_ref):
        return (i if order is None else order_ref[i], j, 0)

    def at_slot(i, j, slots_ref, order_ref):
        return (slots_ref[slot_at + i], j, 0)

    shape = (1, part, width)
    return pl.pallas_call(
        kernel,
        out_shape=jax.ShapeDtypeStruct(acc.shape, acc.dtype),
        grid_spec=pltpu.PrefetchScalarGridSpec(
            num_scalar_prefetch=2,
            grid=(count, block // part),
            in_specs=[pl.BlockSpec(shape, at_tile), pl.BlockSpec(shape, at_slot)],
            out_specs=pl.BlockSpec(shape, at_slot),
        ),
        input_output_aliases={3: 0},
        cost_estimate=pl.CostEstimate(flops=0, bytes_accessed=12 * count * block * width, transcendentals=0),
        name="settle",
    )(slots, slots if order is None else order, source, acc)


def shards(rhs_atlas, tile_block, panels, diag_inverse):
    rows = lax.axis_size("row")
    me = lax.axis_index("row").astype(jnp.int32)
    block = diag_inverse.shape[1]
    width = rhs_atlas.shape[1]
    local = rhs_atlas.shape[0] // block
    share = local // rows
    depth = panels.shape[1]
    half = block // 2
    tiles = rhs_atlas.reshape(local, block, width)

    keep, give, sent0, order, slots = opening(rows, 2, tiles, tile_block, panels, me[None])
    arrived = []

    def travel(part, sent, *events):
        if events:
            sent = after(sent, *events)
        got = lax.ppermute(sent, "row", ring(rows, part[0]))
        arrived.append((part, got))
        return got

    shifts = [2, 1] + list(range(3, rows))
    rounds = [[(2, 0, 1)], [(1, 0, 1)] + [(shift, 0, 1) for shift in shifts[2:]], [(shift, 1, 2) for shift in shifts]]
    last = [(shift, 2, share) for shift in shifts if share > 2]
    if last and share > 3:
        last[-1:] = [(rows - 1, 2, share - 1), (rows - 1, share - 1, share)]
    rounds.append(last)
    plan = sum(rounds[1:], [])
    sents = pack(plan, share, tiles, order)
    sent_of = dict(zip(plan, sents))
    sent_of[rounds[0][0]] = sent0

    def go(number, *events):
        return [travel(part, sent_of[part], *events) for part in rounds[number]]

    factor = lax.all_gather(panels, "col", axis=1, tiled=True)

    done = go(0)
    swap = lax.ppermute(give, "row", partners(rows, 1))
    keep = after(keep + swap, *done, *sents)
    done = go(1, keep)
    bit = 2
    while bit < rows:
        keep = keep + lax.ppermute(keep, "row", partners(rows, bit))
        bit *= 2
    keep = after(keep, *done)
    done = go(2, keep)
    other = lax.ppermute(keep, "row", partners(rows, 1))
    other = after(other, factor, *done)
    go(3, other)
    bit0 = me & 1
    low = jnp.where(bit0 == 0, keep, other)
    high = jnp.where(bit0 == 0, other, keep)
    raw = [jnp.concatenate([low[p * half : (p + 1) * half], high[p * half : (p + 1) * half]], axis=0) for p in range(2)]
    corner = jnp.concatenate([low[2 * half :], high[2 * half :]], axis=0)
    corner = corner.reshape(block // width, depth, width).transpose(1, 0, 2).reshape(depth, block)
    corner = lax.all_gather(corner, "col", axis=0, tiled=True)

    first = mul(diag_inverse[0], raw[0], HIGHEST)
    second = mul(diag_inverse[1], raw[1] - mul_t(corner, first, HIGHEST), HIGHEST)
    block_of_row = jnp.arange(local * block, dtype=jnp.int32)[:, None] // block * rows + me
    acc = jnp.where(block_of_row > 0, mul_t(factor[0], first, HIGH), 0.0)
    acc = acc + jnp.where(block_of_row > 1, mul_t(factor[1], second, HIGH), 0.0)
    acc = acc.reshape(local, block, width)

    acc = settle(acc, tiles, slots, 0, share, order)
    for (shift, lo, hi), got in arrived:
        acc = settle(acc, got, slots, shift * share + lo, hi - lo)
    return jnp.stack([first, second]), acc.reshape(local * block, width)


def solution(mesh):
    placed = (P("row", "col"), P(), P(None, "col", "row"), P())
    return jax.shard_map(
        shards,
        mesh=mesh,
        in_specs=placed,
        out_specs=(P(None, None, "col"), P("row", "col")),
        check_vma=False,
    )
```

time: 777 us -> 456 us (0.59)
  waiting for transfers between devices: 536 us -> 278 us
  matrix products: 134 us -> 56.9 us
  Pallas kernels: 0 us -> 55.7 us
  other arithmetic: 31.2 us -> 7.01 us
  local copies, waits for them, and re-layouts: 43.5 us -> 27.3 us
    all_to_all x1 -> x0, waiting for transfers between devices: 356 us -> none  [shards(): lax.all_to_all(outgoing, 'row', split_axis=0, concat_axis=0, tiled=True)]
    ppermute x0 -> x13, waiting for transfers between devices: none -> 265 us  [the longest x10 161 us: travel(): got = lax.ppermute(sent, 'row', ring(rows, part[0]))]
    psum x2 -> x0, waiting for transfers between devices: 99.3 us -> none  [from_root(): return lax.psum(jnp.where(mine, x, jnp.zeros_like(x)), axis)]
    dot_general x4 -> x5, matrix products: 134 us -> 56.9 us  [the longest x3 48.8 us: mul_t(): lax.dot_general(a, b, (((0,), (0,)), ((), ())), precision=precision, pref...]
    all_gather x2, waiting for transfers between devices: 80.7 us -> 12.3 us  [the longest x1 12.3 us: shards(): corner = lax.all_gather(corner, 'col', axis=0, tiled=True)]
    pallas_call x0 -> x13, Pallas kernels: none -> 55.7 us  [the longest x11 42.8 us: settle(): pl.pallas_call(kernel, out_shape=jax.ShapeDtypeStruct(acc.shape, acc.dtyp...]
    gather x3 -> x0, local copies, waits for them, and re-layouts: 29.2 us -> none  [the longest x1 14.3 us: shards(): outgoing = jnp.take(tiles, send_order, axis=0)]
    select_n x8 -> x1, other arithmetic: 20.6 us -> 1.83 us  [shards(): low = jnp.where(bit0 == 0, keep, other)]
  transfers between devices with their start and end apart: 5 -> 15, of which waited for: 5 -> 11; matrix products, arithmetic and copies ran while one was open for 2% -> 19% of each run, Pallas kernels for 0% -> 12%
where the time goes in v1:
time: 456 us; the launch traced here: 454 us
  waiting for transfers between devices  278 us (61%)
  matrix products  56.9 us (12%)
  Pallas kernels  55.7 us (12%)
  local copies, waits for them, and re-layouts  27.3 us (6%)
  starting transfers between devices  15 us (3%)
  between operations  14.2 us (3%)
  other arithmetic  7.01 us (2%)
    ppermute x10, waiting for transfers between devices, travel(): got = lax.ppermute(sent, 'row', ring(rows, part[0]))  161 us
    ppermute x1, waiting for transfers between devices, shards(): keep = keep + lax.ppermute(keep, 'row', partners(rows, bit))  68.8 us
    dot_general x3, matrix products, mul_t(): lax.dot_general(a, b, (((0,), (0,)), ((), ())), precision=precision, pref...  48.8 us
    pallas_call x11, Pallas kernels, settle(): pl.pallas_call(kernel, out_shape=jax.ShapeDtypeStruct(acc.shape, acc.dtyp...  42.8 us
    ppermute x1, waiting for transfers between devices, shards(): swap = lax.ppermute(give, 'row', partners(rows, 1))  35 us
    add x1, local copies, waits for them, and re-layouts, shards(): acc = acc + jnp.where(block_of_row > 1, mul_t(factor[1], second, HIGH), 0.0)  17.4 us
    ppermute x10, starting transfers between devices, travel(): got = lax.ppermute(sent, 'row', ring(rows, part[0]))  13.2 us
    all_gather x1, waiting for transfers between devices, shards(): corner = lax.all_gather(corner, 'col', axis=0, tiled=True)  12.3 us
  transfers between devices with their start and end apart: 15, of which 11 were waited for; matrix products, arithmetic and copies ran while one was open for 19% of the time, Pallas kernels for 12%

profile of v1, /device:TPU:18, one launch (start us, length us, event | category | flops | bytes accessed | tf_op | source)
XLA Modules:
  0.0 454.3 jit_solution(4383479590228154491)
XLA Ops:
  7.2 0.7 all-gather.3.cloned.1.call-update
  7.9 5.0 %opening.1 = (f32[544,512]{1,0:T(8,128)}, f32[544,512]{1,0:T(8,128)}, f32[1,512,512]{2,1,0:T(8,128)}, s32[16]{0:T(128)}, s32[24]{0:T(128)}) custom-call(s32[64]{0:T(128)} %block_ref.1, s32[1]{0:T(128)} %bitcast.me_ref, f32[16,512,512]{2,1,0:T(8,128)} %bitcast.33, f32[2,64,8192]{2,1,0:T(8,128)} %panels_ref.1), custom_call_target="tpu_custom_call" | custom-call | bytes 6291456 | tf_op jit(solution)/shard_map/opening/pallas_call | solution.py:154
  13.0 1.1 collective-permute-start
  14.1 0.8 collective-permute-start.1
  15.5 7.9 %pack.1 = (f32[1,512,512]{2,1,0:T(8,128)S(1)}, f32[1,512,512]{2,1,0:T(8,128)S(1)}, f32[1,512,512]{2,1,0:T(8,128)}, f32[1,512,512]{2,1,0:T(8,128)}, f32[1,512,512...) custom-call(s32[16]{0:T(128)S(1)} %copy-done, ...), custom_call_target="tpu_custom_call" | custom-call | bytes 23068672 | tf_op jit(solution)/shard_map/pack/pallas_call | solution.py:198
  23.4 1.3 copy-done.1
  24.7 1.0 copy-done.2
  25.7 35.0 %collective-permute-done = f32[544,512]{1,0:T(8,128)S(1)} collective-permute-done((f32[544,512]{1,0:T(8,128)}, f32[544,512]{1,0:T(8,128)S(1)}, u32[]{:S(2)}, u32[]{:S(2)}) %collective-permute-start) | collective-permute-done | bytes 1114144 | tf_op jit(solution)/shard_map/ppermute | solution.py:277
  60.9 0.9 collective-permute-done.1.tile_ref
  62.4 2.4 collective-permute-start.4
  64.9 68.8 %collective-permute-done.2 = f32[544,512]{1,0:T(8,128)S(1)} collective-permute-done((f32[544,512]{1,0:T(8,128)S(1)}, f32[544,512]{1,0:T(8,128)S(1)}, u32[]{:S(2)}, u32[]{:S(2)}) %collective-permute-start.2) | collective-permute-done | bytes 1114144 | tf_op jit(solution)/shard_map/ppermute | solution.py:282
  133.8 1.2 add.36
  135.0 19.6 %collective-permute-done.4.tile_ref = f32[1,512,512]{2,1,0:T(8,128)S(1)} collective-permute-done((f32[1,512,512]{2,1,0:T(8,128)S(1)}, f32[1,512,512]{2,1,0:T(8,128)S(1)}, u32[]{:S(2)}, u32[]{:S(2)}) %collective-permute-start.4) | collective-permute-done | bytes 1048608 | tf_op jit(solution)/shard_map/ppermute | solution.py:256
  154.6 2.4 collective-permute-done.3.tile_ref
  157.0 1.1 collective-permute-start.8
  158.1 1.0 collective-permute-start.7
  159.1 2.3 collective-permute-start.6
  161.4 45.8 %collective-permute-done.8.tile_ref = f32[1,512,512]{2,1,0:T(8,128)} collective-permute-done((f32[1,512,512]{2,1,0:T(8,128)}, f32[1,512,512]{2,1,0:T(8,128)}, u32[]{:S(2)}, u32[]{:S(2)}) %collective-permute-start.8) | collective-permute-done | bytes 1048608 | tf_op jit(solution)/shard_map/ppermute | solution.py:256
  207.2 41.4 %collective-permute-done.7.tile_ref = f32[1,512,512]{2,1,0:T(8,128)} collective-permute-done((f32[1,512,512]{2,1,0:T(8,128)}, f32[1,512,512]{2,1,0:T(8,128)}, u32[]{:S(2)}, u32[]{:S(2)}) %collective-permute-start.7) | collective-permute-done | bytes 1048608 | tf_op jit(solution)/shard_map/ppermute | solution.py:256
  248.5 1.8 collective-permute-done.6.tile_ref
  250.3 1.8 broadcast_select_fusion.1
  252.2 1.0 copy-done.4
  253.5 0.7 pad_maximum_fusion.1
  254.5 3.8 collective-permute-start.11
  258.3 1.6 collective-permute-start.9
  259.8 2.7 fusion.19
  262.6 4.5 fusion.2
  267.1 12.3 %all-gather.5.cloned.1.call-done = f32[512,512]{1,0:T(8,128)} async-done(((f32[64,512]{1,0:T(8,128)}), f32[512,512]{1,0:T(8,128)}) %all-gather.5.cloned.1.call-update) | async-done | bytes 1048592 | tf_op jit(solution)/shard_map/all_gather | solution.py:295
  279.4 5.5 %convolution_subtract_fusion = f32[512,512]{1,0:T(8,128)S(1)} fusion(f32[512,512]{1,0:T(8,128)} %all-gather.5.cloned.1.call-done, f32[512,512]{1,0:T(8,128)} %fusion.2, f32[256,512]{1,0:T(8,128)} %get-tuple-element.65, f32[256,512]{1,0:T(8,128)} %get-tuple-element.58), kind=kOutput, calls=%fused_computation.6 | convolution fusion | flops 1611137024 | bytes 4194304 | tf_op jit(solution)/shard_map/dot_general | solution.py:31
  284.8 3.6 fusion.6
  288.4 21.1 %fusion = f32[512,8192]{1,0:T(8,128)} fusion(f32[512,512]{1,0:T(8,128)S(1)} %fusion.6, f32[2,512,8192]{2,1,0:T(8,128)} %all-gather.3.cloned.1.call-done), kind=kOutput, calls=%fused_computation.1 | convolution fusion | flops 12884901888 | bytes 34603008 | tf_op jit(solution)/shard_map/dot_general | solution.py:31
  309.5 22.3 %add_bitcast_fusion = f32[8192,512]{0,1:T(8,128)} fusion(f32[512,8192]{1,0:T(8,128)} %fusion, f32[512,512]{1,0:T(8,128)} %fusion.2, f32[2,512,8192]{2,1,0:T(8,128)} %all-gather.3.cloned.1.call-done, pred[8192]{0:T(1024)(128)(4,1)S(1)} %get-tuple-element.62, pred[8192]{0:T(1024)(128)(4,1)S(1)} %get-tuple-element.63), kind=kOutput, calls=%fused_computation.4 | convolution fusion | flops 12897484800 | bytes 51396608 | tf_op jit(solution)/shard_map/dot_general | solution.py:31
  331.8 17.4 %copy.17 = f32[8192,512]{1,0:T(8,128)} copy(f32[8192,512]{0,1:T(8,128)} %add_bitcast_fusion) | data formatting | bytes 33554432 | tf_op jit(solution)/shard_map/add | solution.py:301
  349.2 3.1 pad_maximum_fusion
  352.3 2.9 copy.18
  355.2 8.3 %settle.11.old_ref = f32[16,512,512]{2,1,0:T(8,128)} custom-call(s32[24]{0:T(128)} %get-tuple-element.49.slots_ref.order_ref, s32[16]{0:T(128)} %get-tuple-element.31.order_ref, f32[16,512,512]{2,1,0:T(8,128)} %bitcast.35, f32[16,512,512]{2,1,0:T(8,128)} %bitcast.31), custom_call_target="tpu_custom_call", output_to_operand_aliasing={{}: (3, {})} | custom-call | bytes 12582912 | tf_op jit(solution)/shard_map/settle/pallas_call | solution.py:224
  363.5 3.1 settle.12.old_ref
  366.6 3.1 settle.13.old_ref
  369.6 3.1 settle.14.old_ref
  372.7 3.1 settle.15.old_ref
  375.8 3.1 settle.16.old_ref
  378.9 3.1 settle.17.old_ref
  382.0 8.8 %collective-permute-done.12.tile_ref = f32[2,512,512]{2,1,0:T(8,128)} collective-permute-done((f32[2,512,512]{2,1,0:T(8,128)}, f32[2,512,512]{2,1,0:T(8,128)}, u32[]{:S(2)}, u32[]{:S(2)}) %collective-permute-start.12) | collective-permute-done | bytes 2097184 | tf_op jit(solution)/shard_map/ppermute | solution.py:256
  390.8 4.9 %settle.18.old_ref = f32[16,512,512]{2,1,0:T(8,128)} custom-call(s32[24]{0:T(128)} %get-tuple-element.49.slots_ref.order_ref, s32[24]{0:T(128)} %get-tuple-element.49.slots_ref.order_ref, f32[2,512,512]{2,1,0:T(8,128)} %collective-permute-done.12.tile_ref, f32[16,512,512]{2,1,0:T(8,128)} %settle.17.old_ref), custom_call_target="tpu_custom_call", output_to_operand_aliasing={{}: (3, {})} | custom-call | bytes 6291456 | tf_op jit(solution)/shard_map/settle/pallas_call | solution.py:224
  395.7 40.7 %collective-permute-done.11.tile_ref = f32[2,512,512]{2,1,0:T(8,128)} collective-permute-done((f32[2,512,512]{2,1,0:T(8,128)S(1)}, f32[2,512,512]{2,1,0:T(8,128)}, u32[]{:S(2)}, u32[]{:S(2)}) %collective-permute-start.11) | collective-permute-done | bytes 2097184 | tf_op jit(solution)/shard_map/ppermute | solution.py:256
  436.3 4.9 %settle.19.old_ref = f32[16,512,512]{2,1,0:T(8,128)} custom-call(s32[24]{0:T(128)} %get-tuple-element.49.slots_ref.order_ref, s32[24]{0:T(128)} %get-tuple-element.49.slots_ref.order_ref, f32[2,512,512]{2,1,0:T(8,128)} %collective-permute-done.11.tile_ref, f32[16,512,512]{2,1,0:T(8,128)} %settle.18.old_ref), custom_call_target="tpu_custom_call", output_to_operand_aliasing={{}: (3, {})} | custom-call | bytes 6291456 | tf_op jit(solution)/shard_map/settle/pallas_call | solution.py:224
  441.2 3.1 settle.20.old_ref
  444.3 3.1 settle.21
  (37 shorter events, 2.3 us)
Async XLA Ops:
  7.2 243.2 %all-gather.3.cloned.1.call-start = ((), (), s32[]{:S(2)}) async-start(), calls=%async_computation | async-start | bytes 37748736 | tf_op jit(solution)/shard_map/all_gather | solution.py:274
  7.9 271.5 %all-gather.5.cloned.1.call-start = ((), (), s32[]{:S(2)}) async-start(), calls=%async_computation.1 | async-start | bytes 1179648 | tf_op jit(solution)/shard_map/all_gather | solution.py:295
  13.0 47.8 %collective-permute-start = (f32[544,512]{1,0:T(8,128)}, f32[544,512]{1,0:T(8,128)S(1)}, u32[]{:S(2)}, u32[]{:S(2)}) collective-permute-start(f32[544,512]{1,0:T(8,128)} %get-tuple-element.29), channel_id=1, source_target_pairs={{0,8},{8,0},{16,24},{24,16},{1,9},{9,1},{17,25},{25,17},{2,10},{10... | collective-permute-start | bytes 3342344 | tf_op jit(solution)/shard_map/ppermute | solution.py:277
  14.1 47.7 %collective-permute-start.1 = (f32[1,512,512]{2,1,0:T(8,128)}, f32[1,512,512]{2,1,0:T(8,128)S(1)}, u32[]{:S(2)}, u32[]{:S(2)}) collective-permute-start(f32[1,512,512]{2,1,0:T(8,128)} %get-tuple-element.30), channel_id=1, source_target_pairs={{0,16},{8,24},{16,0},{24,8},{1,17},{9,25},{17,1},{25,9},{2,18},{10... | collective-permute-start | bytes 3145736 | tf_op jit(solution)/shard_map/ppermute | solution.py:256
  14.9 0.6 copy-start
  15.5 45.2 %copy-start.8 = (f32[544,512]{1,0:T(8,128)S(1)}, f32[544,512]{1,0:T(8,128)}, u32[]{:S(2)}) copy-start(f32[544,512]{1,0:T(8,128)} %get-tuple-element.28) | copy-start | bytes 3342340
  23.4 1.3 copy-start.1
  24.7 1.0 copy-start.2
  61.8 95.1 %copy-start.9 = (f32[1,512,512]{2,1,0:T(8,128)}, f32[1,512,512]{2,1,0:T(8,128)S(1)}, u32[]{:S(2)}) copy-start(f32[1,512,512]{2,1,0:T(8,128)S(1)} %collective-permute-done.1.tile_ref) | copy-start | bytes 3145732
  61.8 71.9 %collective-permute-start.2 = (f32[544,512]{1,0:T(8,128)S(1)}, f32[544,512]{1,0:T(8,128)S(1)}, u32[]{:S(2)}, u32[]{:S(2)}) collective-permute-start(f32[544,512]{1,0:T(8,128)S(1)} %add.35), channel_id=1, source_target_pairs={{0,16},{8,24},{16,0},{24,8},{1,17},{9,25},{17,1},{25,9},{2,18},{10... | collective-permute-start | bytes 3342344 | tf_op jit(solution)/shard_map/ppermute | solution.py:282
  62.4 92.2 %collective-permute-start.4 = (f32[1,512,512]{2,1,0:T(8,128)S(1)}, f32[1,512,512]{2,1,0:T(8,128)S(1)}, u32[]{:S(2)}, u32[]{:S(2)}) collective-permute-start(f32[1,512,512]{2,1,0:T(8,128)S(1)} %get-tuple-element.43), channel_id=1, source_target_pairs={{0,24},{8,0},{16,8},{24,16},{1,25},{9,1},{17,9},{25,17},{2,26},{10... | collective-permute-start | bytes 3145736 | tf_op jit(solution)/shard_map/ppermute | solution.py:256
  64.9 92.1 %collective-permute-start.3 = (f32[1,512,512]{2,1,0:T(8,128)S(1)}, f32[1,512,512]{2,1,0:T(8,128)S(1)}, u32[]{:S(2)}, u32[]{:S(2)}) collective-permute-start(f32[1,512,512]{2,1,0:T(8,128)S(1)} %get-tuple-element.42), channel_id=1, source_target_pairs={{0,8},{8,16},{16,24},{24,0},{1,9},{9,17},{17,25},{25,1},{2,10},{10... | collective-permute-start | bytes 3145736 | tf_op jit(solution)/shard_map/ppermute | solution.py:256
  154.6 2.4 copy-start.10
  157.0 1.1 copy-start.11
  157.0 93.3 %collective-permute-start.5 = (f32[544,512]{1,0:T(8,128)}, f32[544,512]{1,0:T(8,128)}, u32[]{:S(2)}, u32[]{:S(2)}) collective-permute-start(f32[544,512]{1,0:T(8,128)} %add.36), channel_id=1, source_target_pairs={{0,8},{8,0},{16,24},{24,16},{1,9},{9,1},{17,25},{25,17},{2,10},{10... | collective-permute-start | bytes 3342344 | tf_op jit(solution)/shard_map/ppermute | solution.py:286
  157.0 50.2 %collective-permute-start.8 = (f32[1,512,512]{2,1,0:T(8,128)}, f32[1,512,512]{2,1,0:T(8,128)}, u32[]{:S(2)}, u32[]{:S(2)}) collective-permute-start(f32[1,512,512]{2,1,0:T(8,128)} %get-tuple-element.47), channel_id=1, source_target_pairs={{0,24},{8,0},{16,8},{24,16},{1,25},{9,1},{17,9},{25,17},{2,26},{10... | collective-permute-start | bytes 3145736 | tf_op jit(solution)/shard_map/ppermute | solution.py:256
  158.1 90.5 %collective-permute-start.7 = (f32[1,512,512]{2,1,0:T(8,128)}, f32[1,512,512]{2,1,0:T(8,128)}, u32[]{:S(2)}, u32[]{:S(2)}) collective-permute-start(f32[1,512,512]{2,1,0:T(8,128)} %get-tuple-element.46), channel_id=1, source_target_pairs={{0,8},{8,16},{16,24},{24,0},{1,9},{9,17},{17,25},{25,1},{2,10},{10... | collective-permute-start | bytes 3145736 | tf_op jit(solution)/shard_map/ppermute | solution.py:256
  159.1 91.2 %collective-permute-start.6 = (f32[1,512,512]{2,1,0:T(8,128)}, f32[1,512,512]{2,1,0:T(8,128)}, u32[]{:S(2)}, u32[]{:S(2)}) collective-permute-start(f32[1,512,512]{2,1,0:T(8,128)} %get-tuple-element.45), channel_id=1, source_target_pairs={{0,16},{8,24},{16,0},{24,8},{1,17},{9,25},{17,1},{25,9},{2,18},{10... | collective-permute-start | bytes 3145736 | tf_op jit(solution)/shard_map/ppermute | solution.py:256
  252.2 1.0 copy-start.4
  252.2 1.3 copy-start.5
  254.2 8.3 %copy-start.6 = (f32[2,512,512]{2,1,0:T(8,128)S(1)}, f32[2,512,512]{2,1,0:T(8,128)}, u32[]{:S(2)}) copy-start(f32[2,512,512]{2,1,0:T(8,128)} %param.7) | copy-start | bytes 6291460
  254.3 136.5 %collective-permute-start.12 = (f32[2,512,512]{2,1,0:T(8,128)}, f32[2,512,512]{2,1,0:T(8,128)}, u32[]{:S(2)}, u32[]{:S(2)}) collective-permute-start(f32[2,512,512]{2,1,0:T(8,128)} %copy-done.1), channel_id=1, source_target_pairs={{0,16},{8,24},{16,0},{24,8},{1,17},{9,25},{17,1},{25,9},{2,18},{10... | collective-permute-start | bytes 6291464 | tf_op jit(solution)/shard_map/ppermute | solution.py:256
  254.5 181.8 %collective-permute-start.11 = (f32[2,512,512]{2,1,0:T(8,128)S(1)}, f32[2,512,512]{2,1,0:T(8,128)}, u32[]{:S(2)}, u32[]{:S(2)}) collective-permute-start(f32[2,512,512]{2,1,0:T(8,128)S(1)} %get-tuple-element.52), channel_id=1, source_target_pairs={{0,8},{8,16},{16,24},{24,0},{1,9},{9,17},{17,25},{25,1},{2,10},{10... | collective-permute-start | bytes 6291464 | tf_op jit(solution)/shard_map/ppermute | solution.py:256
  258.3 183.0 %collective-permute-start.10 = (f32[1,512,512]{2,1,0:T(8,128)}, f32[1,512,512]{2,1,0:T(8,128)}, u32[]{:S(2)}, u32[]{:S(2)}) collective-permute-start(f32[1,512,512]{2,1,0:T(8,128)} %copy-done.2), channel_id=1, source_target_pairs={{0,24},{8,0},{16,8},{24,16},{1,25},{9,1},{17,9},{25,17},{2,26},{10... | collective-permute-start | bytes 3145736 | tf_op jit(solution)/shard_map/ppermute | solution.py:256
  258.3 186.1 %collective-permute-start.9 = (f32[1,512,512]{2,1,0:T(8,128)S(1)}, f32[1,512,512]{2,1,0:T(8,128)}, u32[]{:S(2)}, u32[]{:S(2)}) collective-permute-start(f32[1,512,512]{2,1,0:T(8,128)S(1)} %get-tuple-element.50), channel_id=1, source_target_pairs={{0,24},{8,0},{16,8},{24,16},{1,25},{9,1},{17,9},{25,17},{2,26},{10... | collective-permute-start | bytes 3145736 | tf_op jit(solution)/shard_map/ppermute | solution.py:256
  279.4 5.5 %copy-start.7 = (f32[2,512,512]{2,1,0:T(8,128)S(1)}, f32[2,512,512]{2,1,0:T(8,128)}, u32[]{:S(2)}) copy-start(f32[2,512,512]{2,1,0:T(8,128)} %param.7) | copy-start | bytes 6291460
  288.4 21.1 %copy-start.3 = (f32[512,512]{1,0:T(8,128)}, f32[512,512]{1,0:T(8,128)S(1)}, u32[]{:S(2)}) copy-start(f32[512,512]{1,0:T(8,128)S(1)} %fusion.6) | copy-start | bytes 3145732
Sparse Core Ops, SparseCore 0:
  9.9 161.8 all-gather.2
  254.3 24.9 all-gather.4
